TPU v7x, 256 devices: a whole 4x4x8 slice. The times are simulated.
256 devices in a mesh: section: 2 (over y_hi), ctx: 16 (over z, core), head: 8 (over x, y_lo).
Axes of the slice: x: 4, y: 4 (y_hi: 2, y_lo: 2; y = y_hi * 2 + y_lo), z: 8, core: 2. Of those that a mesh axis runs over, the one named last changes fastest.
Arguments:
- queries: bfloat16 [2, 4096, 6144], P('section', ('ctx', 'head'))
- noisy_keys: bfloat16 [2, 4096, 1024], P('section', ('ctx', 'head'))
- noisy_values: bfloat16 [2, 4096, 1024], P('section', ('ctx', 'head')), may hold values from -6 to 6
- clean_keys: bfloat16 [2, 4096, 1024], P('section', ('ctx', 'head')), may hold values from -6 to 6
- clean_values: bfloat16 [2, 4096, 1024], P('section', ('ctx', 'head')), may hold values from -6 to 6
- clip_order: int32 [2], replicated, may hold values from 0 to 1, each once
- key_counts: int32 [2, 32], replicated, may hold values from 2 to 128, as said below
- tile_mask: int32 [2, 32, 32], replicated, may hold values from 0 to 1, as said below
Outputs:
- attended: bfloat16 [2, 4096, 6144], P('section', ('ctx', 'head'))
Inputs may be any that keep to these rules, and one draw needn't show every extreme that they name: `clip_order`: the two sections hold different clips; the smaller number is the earlier clip. The tiles of a clip fall into consecutive frame groups of one or more tiles, with two groups or more; key_counts is 128 in every tile but the last of a group, and 2 to 128 in the last tile of a group (padding at its end); the valid tokens of a tile come first in it; some tile holds 128 valid tokens and some holds 2. With the frame groups of key_counts numbered in order, tile_mask[s, i, j] = 1 exactly when the group of tile j is not later than the group of tile i.
All inputs are finite; a program needn't handle non-finite values.
Results may differ from a plain program's by a relative error of at most 0.007.
Values may be sent and summed in bfloat16 or wider, within the bound.
A program may use at most 64 MiB of HBM per device.

v0:
```python
import functools
import math

import jax
import jax.numpy as jnp
from jax import lax
from jax.experimental import pallas as pl
from jax.experimental.pallas import tpu as pltpu
from jax.sharding import PartitionSpec as P

MESH = pl.DeviceIdType.MESH
HD = 128
TILE = 128
CLOSED = -1e30
EXP_SCALE = math.log2(math.e) * HD ** -0.5


def remote(src, dst, send_sem, recv_sem, device):
    return pltpu.make_async_remote_copy(
        src_ref=src,
        dst_ref=dst,
        send_sem=send_sem,
        recv_sem=recv_sem,
        device_id=device,
        device_id_type=MESH,
    )


def kernel(
    dims,
    order_hbm,
    counts_hbm,
    mask_hbm,
    q_ref,
    nk_ref,
    nv_ref,
    ck_ref,
    cv_ref,
    out_ref,
    order_ref,
    counts_ref,
    mask_ref,
    stage_kv,
    stage_q,
    qbuf,
    qcat,
    kv,
    kx,
    acc,
    run_max,
    score_a,
    score_b,
    max_a,
    max_b,
    obuf,
    load_sem,
    kv_send,
    kv_recv,
    q_send,
    q_recv,
    ring_send,
    ring_recv,
    out_send,
    out_recv,
):
    n_ctx, n_head, rows, per_group = dims
    chips = n_ctx // 2
    half = chips // 2
    block = rows * n_head
    pair_keys = 2 * block
    q_cols = per_group * HD
    tiles = block // TILE
    s = lax.axis_index("section")
    c = lax.axis_index("ctx")
    h = lax.axis_index("head")
    other = 1 - s
    z = c // 2
    core = c % 2
    sib = (s, 2 * z + 1 - core, h)
    up = (s, lax.rem(c + 2, n_ctx), h)
    down = (s, lax.rem(c + n_ctx - 2, n_ctx), h)

    def peer(d):
        return lax.rem(h + d, n_head)

    def head_rows(number):
        return pl.ds(pl.multiple_of(number * rows, rows), rows)

    def head_cols(number, width):
        return pl.ds(pl.multiple_of(number * width, width), width)

    def block_rows(number):
        return pl.ds(pl.multiple_of(number * block, block), block)

    loads = [
        pltpu.make_async_copy(ref.at[0], stage_kv.at[a], load_sem.at[a])
        for a, ref in enumerate((nk_ref, nv_ref, ck_ref, cv_ref))
    ]
    loads.append(pltpu.make_async_copy(q_ref.at[0], stage_q, load_sem.at[4]))
    tables = ((order_hbm, order_ref), (counts_hbm, counts_ref), (mask_hbm, mask_ref))
    for a, (src, dst) in enumerate(tables):
        loads.append(pltpu.make_async_copy(src, dst, load_sem.at[5 + a]))
    for copy in loads:
        copy.start()

    barrier = pltpu.get_barrier_semaphore()
    greeted = [(s, c, peer(d)) for d in range(1, n_head)]
    greeted += [(other, c, peer(d)) for d in range(n_head)]
    greeted += [sib, up, down]
    for device in greeted:
        pl.semaphore_signal(barrier, inc=1, device_id=device, device_id_type=MESH)
    for copy in loads[:4]:
        copy.wait()
    pl.semaphore_wait(barrier, len(greeted))

    mine = pl.ds(pl.multiple_of(c * block + h * rows, rows), rows)
    sends = []

    def send_kv(part, d, device):
        copy = remote(
            stage_kv.at[2 * part:2 * part + 2, :, head_cols(peer(d), HD)],
            kv.at[2 * part:2 * part + 2, mine, :],
            kv_send.at[part, d],
            kv_recv.at[part],
            device,
        )
        copy.start()
        sends.append(copy)

    for d in range(1, n_head):
        send_kv(0, d, (s, c, peer(d)))
    pltpu.make_async_copy(
        stage_kv.at[0:2, :, head_cols(h, HD)], kv.at[0:2, mine, :], kv_recv.at[0]
    ).start()
    for d in range(n_head):
        send_kv(1, d, (other, c, peer(d)))

    loads[4].wait()
    q_mine = head_rows(h)
    for d in range(1, n_head):
        copy = remote(
            stage_q.at[:, head_cols(peer(d), q_cols)],
            qbuf.at[q_mine, :],
            q_send.at[d],
            q_recv,
            (s, c, peer(d)),
        )
        copy.start()
        sends.append(copy)
    pltpu.make_async_copy(
        stage_q.at[:, head_cols(h, q_cols)], qbuf.at[q_mine, :], q_recv
    ).start()

    def part_view(b, part):
        return kv.at[pl.ds(2 * part, 2), block_rows(b), :]

    def ring_copy(b, part, device, slot):
        view = part_view(b, part)
        return remote(view, view, ring_send.at[slot], ring_recv.at[b, part], device)

    def arrived(b, part):
        view = part_view(b, part)
        pltpu.make_async_copy(view, view, ring_recv.at[b, part]).wait()

    def slot_of(part, way, i):
        return (part * 4 + way) * (half + 1) + i

    def pass_on(i, part, came_up):
        if came_up:
            b = lax.rem(c + n_ctx - 2 * i, n_ctx)
            arrived(b, part)
            if i < half - 1 or (i == half - 1 and part == 0):
                ring_copy(b, part, up, slot_of(part, 0, i)).start()
            ring_copy(b, part, sib, slot_of(part, 2, i)).start()
        else:
            b = lax.rem(c + 2 * i, n_ctx)
            arrived(b, part)
            if i < half - 1 or (i == half - 1 and part == 1):
                ring_copy(b, part, down, slot_of(part, 1, i)).start()
            ring_copy(b, part, sib, slot_of(part, 3, i)).start()

    def pass_both(number):
        i, part = (number + 1) // 2, (number + 1) % 2
        pass_on(i, part, True)
        pass_on(i, part if i < half else 1, False)

    def sib_arrived(delta, part):
        chip = lax.rem(z + delta + chips, chips)
        arrived(2 * chip + 1 - core, part)

    for part in range(2):
        view = part_view(c, part)
        pltpu.make_async_copy(view, view, kv_recv.at[part]).wait()
        for way, device in ((0, up), (1, down), (2, sib)):
            ring_copy(c, part, device, slot_of(part, way, 0)).start()

    lane = lax.broadcasted_iota(jnp.int32, (TILE, HD), 1)
    row = lax.broadcasted_iota(jnp.int32, (TILE, HD), 0)
    for head in range(per_group):
        for t in range(tiles):
            first = head * block + t * TILE
            qcat[first:first + TILE, HD:] = jnp.where(lane == t, 1.0, 0.0).astype(jnp.bfloat16)
    acc[...] = jnp.zeros_like(acc)
    run_max[...] = jnp.full_like(run_max, CLOSED)
    for copy in loads[5:]:
        copy.wait()
    far_order = jnp.full((TILE, HD), order_ref[other], jnp.int32)
    own_order = jnp.full((TILE, HD), order_ref[s], jnp.int32)
    earlier = jnp.where(far_order < own_order, 1, 0)

    def mask_tile(k, _):
        at = pl.ds(pl.multiple_of(k * TILE, TILE), TILE)
        seen = jnp.zeros((TILE, HD), jnp.int32)
        for t in range(tiles):
            seen = jnp.where(lane == t, mask_ref[s, tiles * c + t, k], seen)
        limit = jnp.where(seen > 0, counts_ref[s, k], 0)
        kx[0, at, :] = jnp.where((lane < tiles) & (row >= limit), CLOSED, 0.0).astype(jnp.bfloat16)
        limit = earlier * counts_ref[other, k]
        kx[1, at, :] = jnp.where((lane < tiles) & (row >= limit), CLOSED, 0.0).astype(jnp.bfloat16)
        return 0

    lax.fori_loop(0, n_ctx * tiles, mask_tile, 0)

    pass_both(1)
    pltpu.make_async_copy(qbuf, qbuf, q_recv).wait()
    for head in range(per_group):
        qcat[head * block:(head + 1) * block, :HD] = qbuf[:, head * HD:(head + 1) * HD]
    sib_arrived(0, 0)
    sib_arrived(0, 1)

    def chunk(k, second):
        i, part = (k + 1) // 2, (k + 1) % 2
        if second:
            alone = (half - i % half) // half
            part = (part + alone) % 2
            chip = lax.rem(z + i, chips)
        else:
            chip = lax.rem(z + chips - i, chips)
        return part, pl.ds(pl.multiple_of(chip * pair_keys, pair_keys), pair_keys)

    def scores(where, score_ref, max_ref):
        part, at = where
        keys = jnp.concatenate([kv[2 * part, at, :], kx[part, at, :]], 1)
        found = lax.dot_general(
            qcat[...], keys, (((1,), (1,)), ((), ())), preferred_element_type=jnp.float32
        )
        score_ref[...] = found
        top = found[:, :HD]
        for t in range(1, pair_keys // HD):
            top = jnp.maximum(top, found[:, t * HD:(t + 1) * HD])
        max_ref[...] = top

    def fold(where, score_ref, max_ref):
        part, at = where
        old = run_max[...]
        new = jnp.maximum(old, jnp.max(max_ref[...], axis=1, keepdims=True))
        factor = jnp.exp2((old - new) * EXP_SCALE)
        run_max[...] = new
        pieces = []
        for t in range(pair_keys // HD):
            piece = score_ref[:, t * HD:(t + 1) * HD]
            pieces.append(jnp.exp2((piece - new) * EXP_SCALE).astype(jnp.bfloat16))
        weights = jnp.concatenate(pieces, 1)
        ones = jnp.ones((pair_keys, HD), jnp.bfloat16)
        values = jnp.concatenate([kv[2 * part + 1, at, :], ones], 1)
        added = jnp.dot(weights, values, preferred_element_type=jnp.float32)
        acc[...] = acc[...] * jnp.concatenate([factor, factor], 1) + added

    scores(chunk(0, False), score_a, max_a)

    def step(k, _):
        for number in range(2, 2 * half):

            @pl.when(k == number - 1)
            def _(number=number):
                pass_both(number)

        for number in range(1, 2 * half):

            @pl.when(k == number)
            def _(number=number):
                if number < 2 * half - 1:
                    sib_arrived((number + 1) // 2, (number + 1) % 2)
                else:
                    sib_arrived(half, 1)

        scores(chunk(k, True), score_b, max_b)
        fold(chunk(k, False), score_a, max_a)

        for number in range(1, 2 * half):

            @pl.when(k == number - 1)
            def _(number=number):
                sib_arrived(-((number + 1) // 2), (number + 1) % 2)

        scores(chunk(lax.rem(k + 1, 2 * half), False), score_a, max_a)
        fold(chunk(k, True), score_b, max_b)
        return 0

    lax.fori_loop(0, 2 * half, step, 0)

    out_cols = head_cols(h, q_cols)

    def finish(there):
        for head in range(per_group):
            at = pl.ds(pl.multiple_of(head * block + there * rows, rows), rows)
            total = acc[at, :]
            obuf[head_rows(there), head * HD:(head + 1) * HD] = (
                total[:, :HD] / total[:, HD:]
            ).astype(jnp.bfloat16)

    for d in range(1, n_head):
        there = peer(d)
        finish(there)
        copy = remote(
            obuf.at[head_rows(there), :],
            out_ref.at[0, :, out_cols],
            out_send.at[d],
            out_recv,
            (s, c, there),
        )
        copy.start()
        sends.append(copy)
    finish(h)
    pltpu.make_async_copy(obuf.at[head_rows(h), :], out_ref.at[0, :, out_cols], out_recv).start()

    for copy in sends:
        copy.wait_send()
    for part in range(2):
        for way in (0, 1):
            for i in range(half if part == way else half - 1):
                ring_copy(c, part, up, slot_of(part, way, i)).wait_send()
        ring_copy(c, part, sib, slot_of(part, 2, 0)).wait_send()
        for i in range(1, half + 1):
            for way in (2, 3):
                if i < half or way == 2 + part:
                    ring_copy(c, part, sib, slot_of(part, way, i)).wait_send()
    pltpu.make_async_copy(out_ref, out_ref, out_recv).wait()


def local(
    queries, noisy_keys, noisy_values, clean_keys, clean_values, clip_order, key_counts, tile_mask
):
    n_ctx = lax.axis_size("ctx")
    n_head = lax.axis_size("head")
    rows = queries.shape[1]
    groups = noisy_keys.shape[2] // HD
    heads = queries.shape[2] // HD
    per_group = heads // groups
    block = rows * n_head
    keys = block * n_ctx
    half = n_ctx // 4
    bf16, f32 = jnp.bfloat16, jnp.float32
    all_rows = per_group * block
    anywhere = pl.BlockSpec(memory_space=pl.ANY)
    return pl.pallas_call(
        functools.partial(kernel, (n_ctx, n_head, rows, per_group)),
        out_shape=jax.ShapeDtypeStruct(queries.shape, queries.dtype),
        in_specs=[anywhere] * 8,
        out_specs=anywhere,
        scratch_shapes=[
            pltpu.SMEM(clip_order.shape, jnp.int32),
            pltpu.SMEM(key_counts.shape, jnp.int32),
            pltpu.SMEM(tile_mask.shape, jnp.int32),
            pltpu.VMEM((4, rows, groups * HD), bf16),
            pltpu.VMEM((rows, heads * HD), bf16),
            pltpu.VMEM((block, per_group * HD), bf16),
            pltpu.VMEM((all_rows, 2 * HD), bf16),
            pltpu.VMEM((4, keys, HD), bf16),
            pltpu.VMEM((2, keys, HD), bf16),
            pltpu.VMEM((all_rows, 2 * HD), f32),
            pltpu.VMEM((all_rows, HD), f32),
            pltpu.VMEM((all_rows, 2 * block), f32),
            pltpu.VMEM((all_rows, 2 * block), f32),
            pltpu.VMEM((all_rows, HD), f32),
            pltpu.VMEM((all_rows, HD), f32),
            pltpu.VMEM((block, per_group * HD), bf16),
            pltpu.SemaphoreType.DMA((8,)),
            pltpu.SemaphoreType.DMA((2, n_head)),
            pltpu.SemaphoreType.DMA((2,)),
            pltpu.SemaphoreType.DMA((n_head,)),
            pltpu.SemaphoreType.DMA,
            pltpu.SemaphoreType.DMA((8 * (half + 1),)),
            pltpu.SemaphoreType.DMA((n_ctx, 2)),
            pltpu.SemaphoreType.DMA((n_head,)),
            pltpu.SemaphoreType.DMA,
        ],
        compiler_params=pltpu.CompilerParams(
            collective_id=0, has_side_effects=True, vmem_limit_bytes=60 * 2**20
        ),
        cost_estimate=pl.CostEstimate(
            flops=4 * all_rows * 2 * keys * HD,
            bytes_accessed=2**22,
            transcendentals=all_rows * 2 * keys,
        ),
        name="attend",
    )(
        clip_order,
        key_counts,
        tile_mask,
        queries,
        noisy_keys,
        noisy_values,
        clean_keys,
        clean_values,
    )


def solution(mesh):
    split = P("section", ("ctx", "head"), None)
    return jax.shard_map(
        local,
        mesh=mesh,
        in_specs=(split,) * 5 + (P(),) * 3,
        out_specs=split,
        check_vma=False,
    )
```

profile of v0, /device:TPU:8, one launch (start us, length us, event | category | flops | bytes accessed | tf_op | source)
XLA Modules:
  0.0 52.5 jit_solution(16818632073111245330)
XLA Ops:
  0.0 50.7 %attend.1 = bf16[1,32,6144]{2,1,0:T(8,128)(2,1)} custom-call(s32[2]{0:T(128)} %order_hbm.1, s32[2,32]{1,0:T(2,128)} %counts_hbm.1, s32[2,32,32]{2,1,0:T(8,128)} %mask_hbm.1, bf16[1,32,6144]{2,1,0:T(8,128)(2,1)} %q_ref.1, bf16[1,32,1024]{2,1,0:T(8,128)(2,1)} %nk_ref.1, bf16[1,32,1024]{2,1,0:T(8,128)(2,1)} %nv_ref.1, bf16[1,32,1024]{2,1,0:T(8,128)(2,1)} %ck_ref.1, ...), custom_call_target="tpu_custom_call" | custom-call | flops 6442450944 | bytes 4194304 | tf_op jit(solution)/shard_map/attend/pallas_call | solution.py:356
  50.7 1.8 %copy.10 = bf16[1,32,6144]{2,1,0:T(8,128)(2,1)} copy(bf16[1,32,6144]{2,1,0:T(8,128)(2,1)} %attend.1) | data formatting | bytes 786432
where the time goes:
time: 52.6 us; the launch traced here: 52.5 us
  Pallas kernels  50.7 us (96%)
  local copies, waits for them, and re-layouts  1.77 us (3%)
    pallas_call x1, Pallas kernels, local(): pl.pallas_call(functools.partial(kernel, (n_ctx, n_head, rows, per_group)...  50.7 us
    unnamed x1, local copies, waits for them, and re-layouts  1.77 us

commit v1 on v0

--- a/solution.py
+++ b/solution.py
@@ -92,15 +92,16 @@
     def block_rows(number):
         return pl.ds(pl.multiple_of(number * block, block), block)
 
-    loads = [
-        pltpu.make_async_copy(ref.at[0], stage_kv.at[a], load_sem.at[a])
-        for a, ref in enumerate((nk_ref, nv_ref, ck_ref, cv_ref))
+    for a, ref in enumerate((nk_ref, nv_ref, ck_ref, cv_ref)):
+        pltpu.make_async_copy(ref.at[0], stage_kv.at[a], load_sem.at[0]).start()
+    load_q = pltpu.make_async_copy(q_ref.at[0], stage_q, load_sem.at[1])
+    load_q.start()
+    load_tables = [
+        pltpu.make_async_copy(order_hbm, order_ref, load_sem.at[2]),
+        pltpu.make_async_copy(counts_hbm, counts_ref, load_sem.at[3]),
+        pltpu.make_async_copy(mask_hbm, mask_ref, load_sem.at[4]),
     ]
-    loads.append(pltpu.make_async_copy(q_ref.at[0], stage_q, load_sem.at[4]))
-    tables = ((order_hbm, order_ref), (counts_hbm, counts_ref), (mask_hbm, mask_ref))
-    for a, (src, dst) in enumerate(tables):
-        loads.append(pltpu.make_async_copy(src, dst, load_sem.at[5 + a]))
-    for copy in loads:
+    for copy in load_tables:
         copy.start()
 
     barrier = pltpu.get_barrier_semaphore()
@@ -109,23 +110,20 @@
     greeted += [sib, up, down]
     for device in greeted:
         pl.semaphore_signal(barrier, inc=1, device_id=device, device_id_type=MESH)
-    for copy in loads[:4]:
-        copy.wait()
+    pltpu.make_async_copy(stage_kv, stage_kv, load_sem.at[0]).wait()
     pl.semaphore_wait(barrier, len(greeted))
 
     mine = pl.ds(pl.multiple_of(c * block + h * rows, rows), rows)
-    sends = []
 
     def send_kv(part, d, device):
         copy = remote(
             stage_kv.at[2 * part:2 * part + 2, :, head_cols(peer(d), HD)],
             kv.at[2 * part:2 * part + 2, mine, :],
-            kv_send.at[part, d],
+            kv_send,
             kv_recv.at[part],
             device,
         )
         copy.start()
-        sends.append(copy)
 
     for d in range(1, n_head):
         send_kv(0, d, (s, c, peer(d)))
@@ -135,64 +133,70 @@
     for d in range(n_head):
         send_kv(1, d, (other, c, peer(d)))
 
-    loads[4].wait()
+    load_q.wait()
     q_mine = head_rows(h)
     for d in range(1, n_head):
         copy = remote(
             stage_q.at[:, head_cols(peer(d), q_cols)],
             qbuf.at[q_mine, :],
-            q_send.at[d],
+            q_send,
             q_recv,
             (s, c, peer(d)),
         )
         copy.start()
-        sends.append(copy)
     pltpu.make_async_copy(
         stage_q.at[:, head_cols(h, q_cols)], qbuf.at[q_mine, :], q_recv
     ).start()
 
-    def part_view(b, part):
+    def view(b, part):
         return kv.at[pl.ds(2 * part, 2), block_rows(b), :]
 
-    def ring_copy(b, part, device, slot):
-        view = part_view(b, part)
-        return remote(view, view, ring_send.at[slot], ring_recv.at[b, part], device)
-
     def arrived(b, part):
-        view = part_view(b, part)
-        pltpu.make_async_copy(view, view, ring_recv.at[b, part]).wait()
-
-    def slot_of(part, way, i):
-        return (part * 4 + way) * (half + 1) + i
-
-    def pass_on(i, part, came_up):
-        if came_up:
-            b = lax.rem(c + n_ctx - 2 * i, n_ctx)
-            arrived(b, part)
-            if i < half - 1 or (i == half - 1 and part == 0):
-                ring_copy(b, part, up, slot_of(part, 0, i)).start()
-            ring_copy(b, part, sib, slot_of(part, 2, i)).start()
-        else:
-            b = lax.rem(c + 2 * i, n_ctx)
-            arrived(b, part)
-            if i < half - 1 or (i == half - 1 and part == 1):
-                ring_copy(b, part, down, slot_of(part, 1, i)).start()
-            ring_copy(b, part, sib, slot_of(part, 3, i)).start()
-
-    def pass_both(number):
-        i, part = (number + 1) // 2, (number + 1) % 2
-        pass_on(i, part, True)
-        pass_on(i, part if i < half else 1, False)
-
-    def sib_arrived(delta, part):
+        pltpu.make_async_copy(view(b, part), view(b, part), ring_recv.at[b, part]).wait()
+
+    def ring_block(i, way):
+        if way == "up":
+            return lax.rem(c + n_ctx - 2 * i, n_ctx)
+        return lax.rem(c + 2 * i, n_ctx)
+
+    plans = {}
+    for i in range(half + 1):
+        for part in range(2):
+            for number, (way, device) in enumerate((("up", up), ("down", down))):
+                if i < half:
+                    plans[way, i, part] = number, device
+                if 0 < i < half or way == "up":
+                    plans["sib", way, i, part] = 2, sib
+
+    def copy_of(*name):
+        number, device = plans[name]
+        way, i, part = name[-3:]
+        b = ring_block(i, way)
+        piece = view(b, part)
+        if name[0] != "sib" and i == half - 1:
+            piece = piece.at[0:1] if way == "up" else piece.at[1:2]
+        return remote(piece, piece, ring_send.at[number], ring_recv.at[b, part], device)
+
+    def spread(i, way, part):
+        for name in ((way, i, part), ("sib", way, i, part)):
+            if name in plans:
+                copy_of(*name).start()
+
+    def from_ring(i, part):
+        for way in ("up", "down"):
+            if ("sib", way, i, part) in plans:
+                arrived(ring_block(i, way), part)
+                spread(i, way, part)
+
+    def from_sib(delta, part):
         chip = lax.rem(z + delta + chips, chips)
         arrived(2 * chip + 1 - core, part)
 
     for part in range(2):
-        view = part_view(c, part)
-        pltpu.make_async_copy(view, view, kv_recv.at[part]).wait()
-        for way, device in ((0, up), (1, down), (2, sib)):
-            ring_copy(c, part, device, slot_of(part, way, 0)).start()
+        both = kv.at[2 * part:2 * part + 2, block_rows(c), :]
+        pltpu.make_async_copy(both, both, kv_recv.at[part]).wait()
+        spread(0, "down", part)
+        spread(0, "up", part)
 
     lane = lax.broadcasted_iota(jnp.int32, (TILE, HD), 1)
     row = lax.broadcasted_iota(jnp.int32, (TILE, HD), 0)
@@ -202,7 +206,7 @@
             qcat[first:first + TILE, HD:] = jnp.where(lane == t, 1.0, 0.0).astype(jnp.bfloat16)
     acc[...] = jnp.zeros_like(acc)
     run_max[...] = jnp.full_like(run_max, CLOSED)
-    for copy in loads[5:]:
+    for copy in load_tables:
         copy.wait()
     far_order = jnp.full((TILE, HD), order_ref[other], jnp.int32)
     own_order = jnp.full((TILE, HD), order_ref[s], jnp.int32)
@@ -221,21 +225,17 @@
 
     lax.fori_loop(0, n_ctx * tiles, mask_tile, 0)
 
-    pass_both(1)
+    from_ring(1, 0)
     pltpu.make_async_copy(qbuf, qbuf, q_recv).wait()
     for head in range(per_group):
         qcat[head * block:(head + 1) * block, :HD] = qbuf[:, head * HD:(head + 1) * HD]
-    sib_arrived(0, 0)
-    sib_arrived(0, 1)
-
-    def chunk(k, second):
-        i, part = (k + 1) // 2, (k + 1) % 2
-        if second:
-            alone = (half - i % half) // half
-            part = (part + alone) % 2
-            chip = lax.rem(z + i, chips)
-        else:
-            chip = lax.rem(z + chips - i, chips)
+    from_sib(0, 0)
+
+    def chunk(n):
+        i, r = (n + 2) // 4, (n + 2) % 4
+        alone = (half - i % half) // half
+        part = (1 - alone) * (r // 2) + alone * (r % 2)
+        chip = lax.rem(z + chips + i * (2 * (r % 2) - 1), chips)
         return part, pl.ds(pl.multiple_of(chip * pair_keys, pair_keys), pair_keys)
 
     def scores(where, score_ref, max_ref):
@@ -266,38 +266,45 @@
         added = jnp.dot(weights, values, preferred_element_type=jnp.float32)
         acc[...] = acc[...] * jnp.concatenate([factor, factor], 1) + added
 
-    scores(chunk(0, False), score_a, max_a)
+    todo = {n: [] for n in range(1, 4 * half)}
+    todo[1] += [functools.partial(from_sib, 0, 1)]
+    for i in range(1, half + 1):
+        first = 4 * i - 2
+        for part in range(2):
+            if i < half:
+                todo[first + 2 * part] += [functools.partial(from_sib, -i, part)]
+                todo[first + 2 * part + 1] += [functools.partial(from_sib, i, part)]
+            else:
+                todo[first + part] += [functools.partial(from_sib, i, part)]
+    ring_at = {2: [(1, 1)], 4: [(2, 0)], 6: [(2, 1)], 8: [(3, 0)], 10: [(3, 1)], 11: [(4, 0)], 13: [(4, 1)]}
+    for n, events in ring_at.items():
+        todo[n] = [functools.partial(from_ring, *event) for event in events] + todo[n]
+    scores(chunk(0), score_a, max_a)
+
+    def prepare(k, odd):
+        for n, actions in todo.items():
+            if n % 2 == odd and n < 4 * half - 1:
+
+                @pl.when(k == (n - odd) // 2)
+                def _(actions=actions):
+                    for action in actions:
+                        action()
 
     def step(k, _):
-        for number in range(2, 2 * half):
-
-            @pl.when(k == number - 1)
-            def _(number=number):
-                pass_both(number)
-
-        for number in range(1, 2 * half):
-
-            @pl.when(k == number)
-            def _(number=number):
-                if number < 2 * half - 1:
-                    sib_arrived((number + 1) // 2, (number + 1) % 2)
-                else:
-                    sib_arrived(half, 1)
-
-        scores(chunk(k, True), score_b, max_b)
-        fold(chunk(k, False), score_a, max_a)
-
-        for number in range(1, 2 * half):
-
-            @pl.when(k == number - 1)
-            def _(number=number):
-                sib_arrived(-((number + 1) // 2), (number + 1) % 2)
-
-        scores(chunk(lax.rem(k + 1, 2 * half), False), score_a, max_a)
-        fold(chunk(k, True), score_b, max_b)
+        prepare(k, 1)
+        scores(chunk(2 * k + 1), score_b, max_b)
+        fold(chunk(2 * k), score_a, max_a)
+        prepare(k + 1, 0)
+        scores(chunk(2 * k + 2), score_a, max_a)
+        fold(chunk(2 * k + 1), score_b, max_b)
         return 0
 
-    lax.fori_loop(0, 2 * half, step, 0)
+    lax.fori_loop(0, 2 * half - 1, step, 0)
+    for action in todo[4 * half - 1]:
+        action()
+    scores(chunk(4 * half - 1), score_b, max_b)
+    fold(chunk(4 * half - 2), score_a, max_a)
+    fold(chunk(4 * half - 1), score_b, max_b)
 
     out_cols = head_cols(h, q_cols)
 
@@ -315,26 +322,25 @@
         copy = remote(
             obuf.at[head_rows(there), :],
             out_ref.at[0, :, out_cols],
-            out_send.at[d],
+            out_send,
             out_recv,
             (s, c, there),
         )
         copy.start()
-        sends.append(copy)
     finish(h)
     pltpu.make_async_copy(obuf.at[head_rows(h), :], out_ref.at[0, :, out_cols], out_recv).start()
 
-    for copy in sends:
-        copy.wait_send()
-    for part in range(2):
-        for way in (0, 1):
-            for i in range(half if part == way else half - 1):
-                ring_copy(c, part, up, slot_of(part, way, i)).wait_send()
-        ring_copy(c, part, sib, slot_of(part, 2, 0)).wait_send()
-        for i in range(1, half + 1):
-            for way in (2, 3):
-                if i < half or way == 2 + part:
-                    ring_copy(c, part, sib, slot_of(part, way, i)).wait_send()
+    def drained(view, sem):
+        pltpu.make_async_copy(view, view, sem).wait()
+
+    away = block - rows
+    drained(kv.at[0:2, 0:2 * block - rows, :], kv_send)
+    drained(qbuf.at[0:away, :], q_send)
+    along = kv.at[:, 0:(2 * half - 1) * block // 2, :]
+    drained(along, ring_send.at[0])
+    drained(along, ring_send.at[1])
+    drained(kv.at[:, 0:chips * block, :], ring_send.at[2])
+    drained(obuf.at[0:away, :], out_send)
     pltpu.make_async_copy(out_ref, out_ref, out_recv).wait()
 
 
@@ -375,14 +381,14 @@
             pltpu.VMEM((all_rows, HD), f32),
             pltpu.VMEM((all_rows, HD), f32),
             pltpu.VMEM((block, per_group * HD), bf16),
-            pltpu.SemaphoreType.DMA((8,)),
-            pltpu.SemaphoreType.DMA((2, n_head)),
+            pltpu.SemaphoreType.DMA((5,)),
+            pltpu.SemaphoreType.DMA,
             pltpu.SemaphoreType.DMA((2,)),
-            pltpu.SemaphoreType.DMA((n_head,)),
             pltpu.SemaphoreType.DMA,
-            pltpu.SemaphoreType.DMA((8 * (half + 1),)),
+            pltpu.SemaphoreType.DMA,
+            pltpu.SemaphoreType.DMA((3,)),
             pltpu.SemaphoreType.DMA((n_ctx, 2)),
-            pltpu.SemaphoreType.DMA((n_head,)),
+            pltpu.SemaphoreType.DMA,
             pltpu.SemaphoreType.DMA,
         ],
         compiler_params=pltpu.CompilerParams(

time: 52.6 us -> 50.6 us (0.962)
  Pallas kernels: 50.7 us -> 48.7 us
    pallas_call x1, Pallas kernels: 50.7 us -> 48.7 us  [local(): pl.pallas_call(functools.partial(kernel, (n_ctx, n_head, rows, per_group)...]
where the time goes in v1:
time: 50.6 us; the launch traced here: 50.5 us
  Pallas kernels  48.7 us (96%)
  local copies, waits for them, and re-layouts  1.77 us (3%)
    pallas_call x1, Pallas kernels, local(): pl.pallas_call(functools.partial(kernel, (n_ctx, n_head, rows, per_group)...  48.7 us
    unnamed x1, local copies, waits for them, and re-layouts  1.77 us

profile of v1, /device:TPU:8, one launch (start us, length us, event | category | flops | bytes accessed | tf_op | source)
XLA Modules:
  0.0 50.5 jit_solution(16978726242448491023)
XLA Ops:
  0.0 48.7 %attend.1 = bf16[1,32,6144]{2,1,0:T(8,128)(2,1)} custom-call(s32[2]{0:T(128)} %order_hbm.1, s32[2,32]{1,0:T(2,128)} %counts_hbm.1, s32[2,32,32]{2,1,0:T(8,128)} %mask_hbm.1, bf16[1,32,6144]{2,1,0:T(8,128)(2,1)} %q_ref.1, bf16[1,32,1024]{2,1,0:T(8,128)(2,1)} %nk_ref.1, bf16[1,32,1024]{2,1,0:T(8,128)(2,1)} %nv_ref.1, bf16[1,32,1024]{2,1,0:T(8,128)(2,1)} %ck_ref.1, ...), custom_call_target="tpu_custom_call" | custom-call | flops 6442450944 | bytes 4194304 | tf_op jit(solution)/shard_map/attend/pallas_call | solution.py:362
  48.7 1.8 %copy.10 = bf16[1,32,6144]{2,1,0:T(8,128)(2,1)} copy(bf16[1,32,6144]{2,1,0:T(8,128)(2,1)} %attend.1) | data formatting | bytes 786432

commit v2 on v1

--- a/solution.py
+++ b/solution.py
@@ -133,21 +133,6 @@
     for d in range(n_head):
         send_kv(1, d, (other, c, peer(d)))
 
-    load_q.wait()
-    q_mine = head_rows(h)
-    for d in range(1, n_head):
-        copy = remote(
-            stage_q.at[:, head_cols(peer(d), q_cols)],
-            qbuf.at[q_mine, :],
-            q_send,
-            q_recv,
-            (s, c, peer(d)),
-        )
-        copy.start()
-    pltpu.make_async_copy(
-        stage_q.at[:, head_cols(h, q_cols)], qbuf.at[q_mine, :], q_recv
-    ).start()
-
     def view(b, part):
         return kv.at[pl.ds(2 * part, 2), block_rows(b), :]
 
@@ -193,6 +178,21 @@
         arrived(2 * chip + 1 - core, part)
 
     for part in range(2):
+        if part == 1:
+            load_q.wait()
+            q_mine = head_rows(h)
+            for d in range(1, n_head):
+                copy = remote(
+                    stage_q.at[:, head_cols(peer(d), q_cols)],
+                    qbuf.at[q_mine, :],
+                    q_send,
+                    q_recv,
+                    (s, c, peer(d)),
+                )
+                copy.start()
+            pltpu.make_async_copy(
+                stage_q.at[:, head_cols(h, q_cols)], qbuf.at[q_mine, :], q_recv
+            ).start()
         both = kv.at[2 * part:2 * part + 2, block_rows(c), :]
         pltpu.make_async_copy(both, both, kv_recv.at[part]).wait()
         spread(0, "down", part)
@@ -361,7 +361,7 @@
     anywhere = pl.BlockSpec(memory_space=pl.ANY)
     return pl.pallas_call(
         functools.partial(kernel, (n_ctx, n_head, rows, per_group)),
-        out_shape=jax.ShapeDtypeStruct(queries.shape, queries.dtype),
+        out_shape=pltpu.VMEM(queries.shape, queries.dtype),
         in_specs=[anywhere] * 8,
         out_specs=anywhere,
         scratch_shapes=[

time: 50.6 us -> 49 us (0.968)
  local copies, waits for them, and re-layouts: 1.77 us -> 0.75 us
  Pallas kernels: 48.7 us -> 48.1 us
    unnamed x1, local copies, waits for them, and re-layouts: 1.77 us -> 0.75 us
    pallas_call x1, Pallas kernels: 48.7 us -> 48.1 us  [local(): pl.pallas_call(functools.partial(kernel, (n_ctx, n_head, rows, per_group)...]
where the time goes in v2:
time: 49 us; the launch traced here: 48.9 us
  Pallas kernels  48.1 us (98%)
  local copies, waits for them, and re-layouts  0.75 us (2%)
    pallas_call x1, Pallas kernels, local(): pl.pallas_call(functools.partial(kernel, (n_ctx, n_head, rows, per_group)...  48.1 us

profile of v2, /device:TPU:8, one launch (start us, length us, event | category | flops | bytes accessed | tf_op | source)
XLA Modules:
  0.0 48.9 jit_solution(8414594403491591993)
XLA Ops:
  0.0 48.1 %attend.1 = bf16[1,32,6144]{2,1,0:T(8,128)(2,1)S(1)} custom-call(s32[2]{0:T(128)} %order_hbm.1, s32[2,32]{1,0:T(2,128)} %counts_hbm.1, s32[2,32,32]{2,1,0:T(8,128)} %mask_hbm.1, bf16[1,32,6144]{2,1,0:T(8,128)(2,1)} %q_ref.1, bf16[1,32,1024]{2,1,0:T(8,128)(2,1)} %nk_ref.1, bf16[1,32,1024]{2,1,0:T(8,128)(2,1)} %nv_ref.1, bf16[1,32,1024]{2,1,0:T(8,128)(2,1)} %ck_ref.1, ...), custom_call_target="tpu_custom_call" | custom-call | flops 6442450944 | bytes 4194304 | tf_op jit(solution)/shard_map/attend/pallas_call | solution.py:362
  48.1 0.7 %copy.10 = bf16[1,32,6144]{2,1,0:T(8,128)(2,1)} copy(bf16[1,32,6144]{2,1,0:T(8,128)(2,1)S(1)} %attend.1) | data formatting | bytes 786432

commit v3 on v2

--- a/solution.py
+++ b/solution.py
@@ -200,10 +200,14 @@
 
     lane = lax.broadcasted_iota(jnp.int32, (TILE, HD), 1)
     row = lax.broadcasted_iota(jnp.int32, (TILE, HD), 0)
-    for head in range(per_group):
-        for t in range(tiles):
-            first = head * block + t * TILE
-            qcat[first:first + TILE, HD:] = jnp.where(lane == t, 1.0, 0.0).astype(jnp.bfloat16)
+    part_rows = rows // 2
+    owners = n_head // tiles
+    half_rows = per_group * TILE
+    tile_of_row = row // (owners * part_rows)
+    for first in range(0, 2 * half_rows, TILE):
+        qcat[first:first + TILE, HD:] = jnp.where(lane == tile_of_row, 1.0, 0.0).astype(
+            jnp.bfloat16
+        )
     acc[...] = jnp.zeros_like(acc)
     run_max[...] = jnp.full_like(run_max, CLOSED)
     for copy in load_tables:
@@ -227,8 +231,14 @@
 
     from_ring(1, 0)
     pltpu.make_async_copy(qbuf, qbuf, q_recv).wait()
-    for head in range(per_group):
-        qcat[head * block:(head + 1) * block, :HD] = qbuf[:, head * HD:(head + 1) * HD]
+    for side in range(2):
+        for head in range(per_group):
+            for owner in range(n_head):
+                to = side * half_rows + head * TILE + owner * part_rows
+                at = owner * rows + side * part_rows
+                qcat[to:to + part_rows, :HD] = qbuf[
+                    at:at + part_rows, head * HD:(head + 1) * HD
+                ]
     from_sib(0, 0)
 
     def chunk(n):
@@ -238,33 +248,33 @@
         chip = lax.rem(z + chips + i * (2 * (r % 2) - 1), chips)
         return part, pl.ds(pl.multiple_of(chip * pair_keys, pair_keys), pair_keys)
 
-    def scores(where, score_ref, max_ref):
+    def scores(where, score_ref, max_ref, side=slice(None)):
         part, at = where
         keys = jnp.concatenate([kv[2 * part, at, :], kx[part, at, :]], 1)
         found = lax.dot_general(
-            qcat[...], keys, (((1,), (1,)), ((), ())), preferred_element_type=jnp.float32
+            qcat[side, :], keys, (((1,), (1,)), ((), ())), preferred_element_type=jnp.float32
         )
-        score_ref[...] = found
+        score_ref[side, :] = found
         top = found[:, :HD]
         for t in range(1, pair_keys // HD):
             top = jnp.maximum(top, found[:, t * HD:(t + 1) * HD])
-        max_ref[...] = top
-
-    def fold(where, score_ref, max_ref):
+        max_ref[side, :] = top
+
+    def fold(where, score_ref, max_ref, side=slice(None)):
         part, at = where
-        old = run_max[...]
-        new = jnp.maximum(old, jnp.max(max_ref[...], axis=1, keepdims=True))
+        old = run_max[side, :]
+        new = jnp.maximum(old, jnp.max(max_ref[side, :], axis=1, keepdims=True))
         factor = jnp.exp2((old - new) * EXP_SCALE)
-        run_max[...] = new
+        run_max[side, :] = new
         pieces = []
         for t in range(pair_keys // HD):
-            piece = score_ref[:, t * HD:(t + 1) * HD]
+            piece = score_ref[side, t * HD:(t + 1) * HD]
             pieces.append(jnp.exp2((piece - new) * EXP_SCALE).astype(jnp.bfloat16))
         weights = jnp.concatenate(pieces, 1)
         ones = jnp.ones((pair_keys, HD), jnp.bfloat16)
         values = jnp.concatenate([kv[2 * part + 1, at, :], ones], 1)
         added = jnp.dot(weights, values, preferred_element_type=jnp.float32)
-        acc[...] = acc[...] * jnp.concatenate([factor, factor], 1) + added
+        acc[side, :] = acc[side, :] * jnp.concatenate([factor, factor], 1) + added
 
     todo = {n: [] for n in range(1, 4 * half)}
     todo[1] += [functools.partial(from_sib, 0, 1)]
@@ -302,33 +312,29 @@
     lax.fori_loop(0, 2 * half - 1, step, 0)
     for action in todo[4 * half - 1]:
         action()
-    scores(chunk(4 * half - 1), score_b, max_b)
-    fold(chunk(4 * half - 2), score_a, max_a)
-    fold(chunk(4 * half - 1), score_b, max_b)
 
     out_cols = head_cols(h, q_cols)
 
-    def finish(there):
+    def finish(number, there):
+        to = pl.ds(pl.multiple_of(there * rows + number * part_rows, part_rows), part_rows)
         for head in range(per_group):
-            at = pl.ds(pl.multiple_of(head * block + there * rows, rows), rows)
-            total = acc[at, :]
-            obuf[head_rows(there), head * HD:(head + 1) * HD] = (
-                total[:, :HD] / total[:, HD:]
-            ).astype(jnp.bfloat16)
-
-    for d in range(1, n_head):
-        there = peer(d)
-        finish(there)
-        copy = remote(
-            obuf.at[head_rows(there), :],
-            out_ref.at[0, :, out_cols],
-            out_send,
-            out_recv,
-            (s, c, there),
-        )
-        copy.start()
-    finish(h)
-    pltpu.make_async_copy(obuf.at[head_rows(h), :], out_ref.at[0, :, out_cols], out_recv).start()
+            first = number * half_rows + head * TILE + there * part_rows
+            total = acc[pl.ds(pl.multiple_of(first, part_rows), part_rows), :]
+            obuf[to, head * HD:(head + 1) * HD] = (total[:, :HD] / total[:, HD:]).astype(
+                jnp.bfloat16
+            )
+        return obuf.at[to, :], out_ref.at[0, number * part_rows:(number + 1) * part_rows, out_cols]
+
+    for number in range(2):
+        side = slice(number * half_rows, (number + 1) * half_rows)
+        scores(chunk(4 * half - 1), score_b, max_b, side)
+        fold(chunk(4 * half - 2), score_a, max_a, side)
+        fold(chunk(4 * half - 1), score_b, max_b, side)
+        for d in range(1, n_head):
+            here, there = finish(number, peer(d))
+            remote(here, there, out_send, out_recv, (s, c, peer(d))).start()
+        here, there = finish(number, h)
+        pltpu.make_async_copy(here, there, out_recv).start()
 
     def drained(view, sem):
         pltpu.make_async_copy(view, view, sem).wait()

time: 49 us -> 47.9 us (0.978)
  Pallas kernels: 48.1 us -> 47.1 us
    pallas_call x1, Pallas kernels: 48.1 us -> 47.1 us  [local(): pl.pallas_call(functools.partial(kernel, (n_ctx, n_head, rows, per_group)...]
where the time goes in v3:
time: 47.9 us; the launch traced here: 47.8 us
  Pallas kernels  47.1 us (98%)
  local copies, waits for them, and re-layouts  0.75 us (2%)
    pallas_call x1, Pallas kernels, local(): pl.pallas_call(functools.partial(kernel, (n_ctx, n_head, rows, per_group)...  47.1 us

profile of v3, /device:TPU:8, one launch (start us, length us, event | category | flops | bytes accessed | tf_op | source)
XLA Modules:
  0.0 47.8 jit_solution(2612368085337848827)
XLA Ops:
  0.0 47.1 %attend.1 = bf16[1,32,6144]{2,1,0:T(8,128)(2,1)S(1)} custom-call(s32[2]{0:T(128)} %order_hbm.1, s32[2,32]{1,0:T(2,128)} %counts_hbm.1, s32[2,32,32]{2,1,0:T(8,128)} %mask_hbm.1, bf16[1,32,6144]{2,1,0:T(8,128)(2,1)} %q_ref.1, bf16[1,32,1024]{2,1,0:T(8,128)(2,1)} %nk_ref.1, bf16[1,32,1024]{2,1,0:T(8,128)(2,1)} %nv_ref.1, bf16[1,32,1024]{2,1,0:T(8,128)(2,1)} %ck_ref.1, ...), custom_call_target="tpu_custom_call" | custom-call | flops 6442450944 | bytes 4194304 | tf_op jit(solution)/shard_map/attend/pallas_call | solution.py:368
  47.1 0.7 %copy.10 = bf16[1,32,6144]{2,1,0:T(8,128)(2,1)} copy(bf16[1,32,6144]{2,1,0:T(8,128)(2,1)S(1)} %attend.1) | data formatting | bytes 786432

commit v4 on v3

--- a/solution.py
+++ b/solution.py
@@ -94,6 +94,12 @@
 
     for a, ref in enumerate((nk_ref, nv_ref, ck_ref, cv_ref)):
         pltpu.make_async_copy(ref.at[0], stage_kv.at[a], load_sem.at[0]).start()
+    barrier = pltpu.get_barrier_semaphore()
+    greeted = [(s, c, peer(d)) for d in range(1, n_head)]
+    greeted += [(other, c, peer(d)) for d in range(n_head)]
+    greeted += [sib, up, down]
+    for device in greeted:
+        pl.semaphore_signal(barrier, inc=1, device_id=device, device_id_type=MESH)
     load_q = pltpu.make_async_copy(q_ref.at[0], stage_q, load_sem.at[1])
     load_q.start()
     load_tables = [
@@ -103,13 +109,6 @@
     ]
     for copy in load_tables:
         copy.start()
-
-    barrier = pltpu.get_barrier_semaphore()
-    greeted = [(s, c, peer(d)) for d in range(1, n_head)]
-    greeted += [(other, c, peer(d)) for d in range(n_head)]
-    greeted += [sib, up, down]
-    for device in greeted:
-        pl.semaphore_signal(barrier, inc=1, device_id=device, device_id_type=MESH)
     pltpu.make_async_copy(stage_kv, stage_kv, load_sem.at[0]).wait()
     pl.semaphore_wait(barrier, len(greeted))
 
@@ -132,6 +131,37 @@
     ).start()
     for d in range(n_head):
         send_kv(1, d, (other, c, peer(d)))
+
+    lane = lax.broadcasted_iota(jnp.int32, (TILE, HD), 1)
+    row = lax.broadcasted_iota(jnp.int32, (TILE, HD), 0)
+    part_rows = rows // 2
+    owners = n_head // tiles
+    half_rows = per_group * TILE
+    tile_of_row = row // (owners * part_rows)
+    for first in range(0, 2 * half_rows, TILE):
+        qcat[first:first + TILE, HD:] = jnp.where(lane == tile_of_row, 1.0, 0.0).astype(
+            jnp.bfloat16
+        )
+    acc[...] = jnp.zeros_like(acc)
+    run_max[...] = jnp.full_like(run_max, CLOSED)
+    for copy in load_tables:
+        copy.wait()
+    far_order = jnp.full((TILE, HD), order_ref[other], jnp.int32)
+    own_order = jnp.full((TILE, HD), order_ref[s], jnp.int32)
+    earlier = jnp.where(far_order < own_order, 1, 0)
+
+    def mask_tile(k, _):
+        at = pl.ds(pl.multiple_of(k * TILE, TILE), TILE)
+        seen = jnp.zeros((TILE, HD), jnp.int32)
+        for t in range(tiles):
+            seen = jnp.where(lane == t, mask_ref[s, tiles * c + t, k], seen)
+        limit = jnp.where(seen > 0, counts_ref[s, k], 0)
+        kx[0, at, :] = jnp.where((lane < tiles) & (row >= limit), CLOSED, 0.0).astype(jnp.bfloat16)
+        limit = earlier * counts_ref[other, k]
+        kx[1, at, :] = jnp.where((lane < tiles) & (row >= limit), CLOSED, 0.0).astype(jnp.bfloat16)
+        return 0
+
+    lax.fori_loop(0, n_ctx * tiles, mask_tile, 0)
 
     def view(b, part):
         return kv.at[pl.ds(2 * part, 2), block_rows(b), :]
@@ -197,37 +227,6 @@
         pltpu.make_async_copy(both, both, kv_recv.at[part]).wait()
         spread(0, "down", part)
         spread(0, "up", part)
-
-    lane = lax.broadcasted_iota(jnp.int32, (TILE, HD), 1)
-    row = lax.broadcasted_iota(jnp.int32, (TILE, HD), 0)
-    part_rows = rows // 2
-    owners = n_head // tiles
-    half_rows = per_group * TILE
-    tile_of_row = row // (owners * part_rows)
-    for first in range(0, 2 * half_rows, TILE):
-        qcat[first:first + TILE, HD:] = jnp.where(lane == tile_of_row, 1.0, 0.0).astype(
-            jnp.bfloat16
-        )
-    acc[...] = jnp.zeros_like(acc)
-    run_max[...] = jnp.full_like(run_max, CLOSED)
-    for copy in load_tables:
-        copy.wait()
-    far_order = jnp.full((TILE, HD), order_ref[other], jnp.int32)
-    own_order = jnp.full((TILE, HD), order_ref[s], jnp.int32)
-    earlier = jnp.where(far_order < own_order, 1, 0)
-
-    def mask_tile(k, _):
-        at = pl.ds(pl.multiple_of(k * TILE, TILE), TILE)
-        seen = jnp.zeros((TILE, HD), jnp.int32)
-        for t in range(tiles):
-            seen = jnp.where(lane == t, mask_ref[s, tiles * c + t, k], seen)
-        limit = jnp.where(seen > 0, counts_ref[s, k], 0)
-        kx[0, at, :] = jnp.where((lane < tiles) & (row >= limit), CLOSED, 0.0).astype(jnp.bfloat16)
-        limit = earlier * counts_ref[other, k]
-        kx[1, at, :] = jnp.where((lane < tiles) & (row >= limit), CLOSED, 0.0).astype(jnp.bfloat16)
-        return 0
-
-    lax.fori_loop(0, n_ctx * tiles, mask_tile, 0)
 
     from_ring(1, 0)
     pltpu.make_async_copy(qbuf, qbuf, q_recv).wait()

time: 47.9 us -> 47.9 us (level)
  no operation moved by 1% of the time
where the time goes in v4:
time: 47.9 us; the launch traced here: 47.8 us
  Pallas kernels  47.1 us (98%)
  local copies, waits for them, and re-layouts  0.75 us (2%)
    pallas_call x1, Pallas kernels, local(): pl.pallas_call(functools.partial(kernel, (n_ctx, n_head, rows, per_group)...  47.1 us

profile of v4, /device:TPU:8, one launch (start us, length us, event | category | flops | bytes accessed | tf_op | source)
XLA Modules:
  0.0 47.8 jit_solution(17584619011980847214)
XLA Ops:
  0.0 47.1 %attend.1 = bf16[1,32,6144]{2,1,0:T(8,128)(2,1)S(1)} custom-call(s32[2]{0:T(128)} %order_hbm.1, s32[2,32]{1,0:T(2,128)} %counts_hbm.1, s32[2,32,32]{2,1,0:T(8,128)} %mask_hbm.1, bf16[1,32,6144]{2,1,0:T(8,128)(2,1)} %q_ref.1, bf16[1,32,1024]{2,1,0:T(8,128)(2,1)} %nk_ref.1, bf16[1,32,1024]{2,1,0:T(8,128)(2,1)} %nv_ref.1, bf16[1,32,1024]{2,1,0:T(8,128)(2,1)} %ck_ref.1, ...), custom_call_target="tpu_custom_call" | custom-call | flops 6442450944 | bytes 4194304 | tf_op jit(solution)/shard_map/attend/pallas_call | solution.py:367
  47.1 0.7 %copy.10 = bf16[1,32,6144]{2,1,0:T(8,128)(2,1)} copy(bf16[1,32,6144]{2,1,0:T(8,128)(2,1)S(1)} %attend.1) | data formatting | bytes 786432

commit v5 on v4

--- a/solution.py
+++ b/solution.py
@@ -326,8 +326,12 @@
 
     for number in range(2):
         side = slice(number * half_rows, (number + 1) * half_rows)
-        scores(chunk(4 * half - 1), score_b, max_b, side)
+        if number == 0:
+            scores(chunk(4 * half - 1), score_b, max_b, side)
         fold(chunk(4 * half - 2), score_a, max_a, side)
+        if number == 0:
+            later = slice(half_rows, 2 * half_rows)
+            scores(chunk(4 * half - 1), score_b, max_b, later)
         fold(chunk(4 * half - 1), score_b, max_b, side)
         for d in range(1, n_head):
             here, there = finish(number, peer(d))

time: 47.9 us -> 47.9 us (level)
  no operation moved by 1% of the time
where the time goes in v5:
time: 47.9 us; the launch traced here: 47.8 us
  Pallas kernels  47.1 us (98%)
  local copies, waits for them, and re-layouts  0.75 us (2%)
    pallas_call x1, Pallas kernels, local(): pl.pallas_call(functools.partial(kernel, (n_ctx, n_head, rows, per_group)...  47.1 us

profile of v5, /device:TPU:8, one launch (start us, length us, event | category | flops | bytes accessed | tf_op | source)
XLA Modules:
  0.0 47.8 jit_solution(15776673672119887326)
XLA Ops:
  0.0 47.1 %attend.1 = bf16[1,32,6144]{2,1,0:T(8,128)(2,1)S(1)} custom-call(s32[2]{0:T(128)} %order_hbm.1, s32[2,32]{1,0:T(2,128)} %counts_hbm.1, s32[2,32,32]{2,1,0:T(8,128)} %mask_hbm.1, bf16[1,32,6144]{2,1,0:T(8,128)(2,1)} %q_ref.1, bf16[1,32,1024]{2,1,0:T(8,128)(2,1)} %nk_ref.1, bf16[1,32,1024]{2,1,0:T(8,128)(2,1)} %nv_ref.1, bf16[1,32,1024]{2,1,0:T(8,128)(2,1)} %ck_ref.1, ...), custom_call_target="tpu_custom_call" | custom-call | flops 6442450944 | bytes 4194304 | tf_op jit(solution)/shard_map/attend/pallas_call | solution.py:371
  47.1 0.7 %copy.10 = bf16[1,32,6144]{2,1,0:T(8,128)(2,1)} copy(bf16[1,32,6144]{2,1,0:T(8,128)(2,1)S(1)} %attend.1) | data formatting | bytes 786432
